TPU v7x, 32 devices: a whole 2x2x4 slice. The times are simulated.
32 devices in a mesh: ctx: 8 (over y, x, core), head: 4 (over z).
Axes of the slice: x: 2, y: 2, z: 4, core: 2. Of those that a mesh axis runs over, the one named last changes fastest.
Arguments:
- queries: bfloat16 [2048, 8192], P('ctx', 'head'), may hold values from -120 to 120, as said below
- keys: bfloat16 [2048, 1024], P(('ctx', 'head')), may hold values from -6 to 6
- values: bfloat16 [2048, 1024], P(('ctx', 'head')), may hold values from -6 to 6
- doc_ids: int32 [2048], replicated, may hold values from 0 to 15, never falling along the last dimension, each value on 1 to 512 neighbouring positions
- output_gradient: bfloat16 [2048, 8192], P('ctx', 'head'), may hold values from -6 to 6
Outputs:
- attended: bfloat16 [2048, 8192], P('ctx', 'head')
- query_grad: bfloat16 [2048, 8192], P('ctx', 'head')
- key_grad: bfloat16 [2048, 1024], P(('ctx', 'head'))
- value_grad: bfloat16 [2048, 1024], P(('ctx', 'head'))
Inputs may be any that keep to these rules, and one draw needn't show every extreme that they name: `queries`: queries lie within -120 to 120 (up to 20 times a key entry), so scores may exceed 200.
All inputs are finite; a program needn't handle non-finite values.
Results may differ from a plain program's by a relative error of at most 0.012.
The roundings to bfloat16 on the way count: a program that leaves them out, or rounds other values in their place, can miss the bound.
Values may be sent and summed in bfloat16 or wider, within the bound.
No kernel may reach another device: no remote copies, remote signals or barrier semaphores. Data moves between devices by JAX's collectives and lax.ppermute only.
A program may use at most 64 MiB of HBM per device.

v0:
```python
import functools
import math

import jax
import jax.numpy as jnp
from jax import lax
from jax.experimental import pallas as pl
from jax.experimental.pallas import tpu as pltpu
from jax.sharding import PartitionSpec as P

HEAD_SIZE = 128
SPAN = 2
TILE = 128
MASKED = -1e30
FIRST = (((0,), (0,)), ((), ()))
LAST = (((1,), (1,)), ((), ()))


def window_kernel(*refs, parts, groups, rows, fold):
    docs_ref, place_ref, start_row = refs[:3]
    earlier = SPAN // fold
    q_refs = refs[3 : 3 + fold]
    g_refs = refs[3 + fold : 3 + 2 * fold]
    at = 3 + 2 * fold
    blocks = refs[at : at + earlier + 1]
    at += earlier + 1
    att_ref, dq_ref = refs[at : at + 2]
    at += 2
    if fold > 1:
        return_ref = refs[at]
        at += 1
    block_grads = refs[at : at + earlier + 1]
    at += earlier + 1
    kw, vw, dk_acc, dv_acc, s_sc, w_sc, ds_sc = refs[at : at + 7]
    if fold > 1:
        q_ref, g_ref, att_sc, dq_sc = refs[at + 7 :]
    else:
        q_ref, g_ref, att_sc, dq_sc = q_refs[0], g_refs[0], att_ref, dq_ref

    step = pl.program_id(1)
    h = place_ref[0]
    side = place_ref[1]
    piece = rows // parts
    block_tiles = rows // TILE
    reach = SPAN * block_tiles
    score_scale = HEAD_SIZE ** -0.5
    factor = score_scale * math.log2(math.e)

    def places(ref_index):
        for f in range(fold):
            base = (ref_index * fold + (jnp.bitwise_xor(side, f) if fold > 1 else 0)) * rows
            for s in range(parts):
                turn = f * rows + lax.rem(h - s + parts, parts) * piece
                yield pl.ds(pl.multiple_of(turn, piece), piece), pl.ds(pl.multiple_of(base + s * piece, piece), piece)

    @pl.when(step == 0)
    def _():
        for b, ref in enumerate(blocks):
            for here, token in places(b):
                kw[token, :] = ref[here, :HEAD_SIZE]
                vw[token, :] = ref[here, HEAD_SIZE:]
        dk_acc[...] = jnp.zeros_like(dk_acc)
        dv_acc[...] = jnp.zeros_like(dv_acc)

    if fold > 1:
        for f in range(fold):
            @pl.when(step // block_tiles == f)
            def _():
                q_ref[...] = q_refs[f][...]
                g_ref[...] = g_refs[f][...]

        query_tile = jnp.bitwise_xor(side, step // block_tiles) * block_tiles + lax.rem(step, block_tiles)
    else:
        query_tile = step
    first = pl.multiple_of((reach + query_tile) * TILE, TILE)
    starts = start_row[0:1, pl.ds(first, TILE)] - first
    key_places = lax.broadcasted_iota(jnp.int32, (TILE, 2 * TILE), 0)
    query_places = lax.rem(lax.broadcasted_iota(jnp.int32, (TILE, 2 * TILE), 1), TILE)

    def attend(tiles):
        low = pl.multiple_of(first - (tiles - 1) * TILE, TILE)
        window = pl.ds(low, tiles * TILE)
        chunks = groups // 2
        tops, inverses, deltas = {}, {}, {}
        both_starts = jnp.concatenate([starts, starts], 1)

        def tile(b):
            return slice(b * TILE, (b + 1) * TILE)

        def folded(x, op):
            return op(x.reshape(TILE // 8, 8, 2 * TILE), axis=0)

        def rows_of(ref, c):
            return jnp.concatenate(
                [ref[:, (2 * c + j) * HEAD_SIZE : (2 * c + j + 1) * HEAD_SIZE] for j in range(2)], 0
            )

        def score(c):
            top = None
            raw = lax.dot_general(kw[window, :], rows_of(q_ref, c), LAST, preferred_element_type=jnp.float32)
            for b in range(tiles):
                s = raw[tile(b)]
                seen = key_places >= both_starts + (tiles - 1 - b) * TILE
                if b == tiles - 1:
                    seen &= key_places <= query_places
                s = jnp.where(seen, s * factor, MASKED)
                s_sc[c, tile(b), :] = s
                high = folded(s, jnp.max)
                top = high if top is None else jnp.maximum(top, high)
            tops[c] = jnp.max(top, axis=0, keepdims=True)

        def weigh(c):
            total = None
            for b in range(tiles):
                e = jnp.exp2(s_sc[c, tile(b), :] - tops[c])
                s_sc[c, tile(b), :] = e
                part = folded(e, jnp.sum)
                total = part if total is None else total + part
            inverses[c] = 1.0 / jnp.sum(total, axis=0, keepdims=True)
            for b in range(tiles):
                w_sc[c, tile(b), :] = (s_sc[c, tile(b), :] * inverses[c]).astype(jnp.bfloat16)

        def gather(c):
            att = lax.dot_general(
                w_sc[c, : tiles * TILE, :], vw[window, :], FIRST, preferred_element_type=jnp.float32
            ).astype(jnp.bfloat16)
            grown = att.astype(jnp.float32) * rows_of(g_ref, c).astype(jnp.float32)
            parts_of = []
            for j in range(2):
                att_sc[:, (2 * c + j) * HEAD_SIZE : (2 * c + j + 1) * HEAD_SIZE] = att[tile(j)]
                parts_of.append(jnp.sum(grown[tile(j)].T, axis=0, keepdims=True))
            deltas[c] = jnp.concatenate(parts_of, 1)

        def differ(c):
            dp = lax.dot_general(vw[window, :], rows_of(g_ref, c), LAST, preferred_element_type=jnp.float32)
            for b in range(tiles):
                p = s_sc[c, tile(b), :] * inverses[c]
                ds_sc[c, tile(b), :] = (p * (dp[tile(b)] - deltas[c])).astype(jnp.bfloat16)

        def spread(c):
            w = w_sc[c, : tiles * TILE, :]
            ds = ds_sc[c, : tiles * TILE, :]
            dq = lax.dot_general(ds, kw[window, :], FIRST, preferred_element_type=jnp.float32)
            dq = (dq * score_scale).astype(jnp.bfloat16)
            for j in range(2):
                dq_sc[:, (2 * c + j) * HEAD_SIZE : (2 * c + j + 1) * HEAD_SIZE] = dq[tile(j)]
            dv_acc[window, :] += jnp.dot(w, rows_of(g_ref, c), preferred_element_type=jnp.float32)
            dk_acc[window, :] += jnp.dot(ds, rows_of(q_ref, c), preferred_element_type=jnp.float32)

        stages = (score, weigh, gather, differ, spread)
        for beat in range(chunks + len(stages) - 1):
            for k, stage in enumerate(stages):
                if 0 <= beat - k < chunks:
                    stage(beat - k)

    here = docs_ref[first]
    tiles = 1
    for j in range(reach):
        tiles = tiles + jnp.where(docs_ref[first - 1 - j * TILE] == here, 1, 0)
    for t in range(1, reach + 2):
        pl.when(tiles == t)(functools.partial(attend, t))

    if fold > 1:
        @pl.when(step < block_tiles)
        def _():
            att_ref[...] = att_sc[...]
            dq_ref[...] = dq_sc[...]

        @pl.when(step >= block_tiles)
        def _():
            return_ref[:, : groups * HEAD_SIZE] = att_sc[...]
            return_ref[:, groups * HEAD_SIZE :] = dq_sc[...]

    @pl.when(step == pl.num_programs(1) - 1)
    def _():
        for b, ref in enumerate(block_grads):
            for here, token in places(b):
                ref[here, :HEAD_SIZE] = (dk_acc[token, :] * score_scale).astype(ref.dtype)
                ref[here, HEAD_SIZE:] = dv_acc[token, :].astype(ref.dtype)


def attention(docs, starts, place, q, g, q_other, g_other, blocks, parts, kv_heads, fold):
    rows = q.shape[0]
    width = q.shape[1] // kv_heads
    total = docs.shape[0]
    block_tiles = rows // TILE
    groups = width // HEAD_SIZE

    def column(n, p):
        return p[1] if fold > 1 else n

    own = pl.BlockSpec((TILE, width), lambda n, s, d, p: (jnp.minimum(s, block_tiles - 1), column(n, p)))
    q_args, g_args, wide = [q], [g], [own]
    out_specs = [own, own]
    out_shape = [pltpu.HBM(q.shape, q.dtype)] * 2
    more_scratch = []
    if fold > 1:
        wide.append(pl.BlockSpec((TILE, width), lambda n, s, d, p: (jnp.maximum(s - block_tiles, 0), column(n, p))))
        q_args.append(q_other)
        g_args.append(g_other)
        out_specs.append(pl.BlockSpec((TILE, 2 * width), lambda n, s, d, p: (jnp.maximum(s - block_tiles, 0), 0)))
        out_shape.append(pltpu.HBM((rows, 2 * width), q.dtype))
        more_scratch = [pltpu.VMEM((TILE, width), q.dtype)] * 4
    block = pl.BlockSpec((fold * rows, 2 * HEAD_SIZE), lambda n, s, d, p: (0, n))
    out_shape += [jax.ShapeDtypeStruct(x.shape, jnp.bfloat16) for x in blocks[:-1]]
    out_shape += [jax.ShapeDtypeStruct(blocks[-1].shape, jnp.float32)]
    window = (total, HEAD_SIZE)
    score_shape = (groups // 2, (SPAN * block_tiles + 1) * TILE, 2 * TILE)
    return pl.pallas_call(
        functools.partial(window_kernel, parts=parts, groups=groups, rows=rows, fold=fold),
        grid_spec=pltpu.PrefetchScalarGridSpec(
            num_scalar_prefetch=2,
            grid=(kv_heads // fold, fold * block_tiles),
            in_specs=[pl.BlockSpec((1, total), lambda n, s, d, p: (0, 0))] + wide * 2 + [block] * len(blocks),
            out_specs=out_specs + [block] * len(blocks),
            scratch_shapes=[
                pltpu.VMEM(window, jnp.bfloat16),
                pltpu.VMEM(window, jnp.bfloat16),
                pltpu.VMEM(window, jnp.float32),
                pltpu.VMEM(window, jnp.float32),
                pltpu.VMEM(score_shape, jnp.float32),
                pltpu.VMEM(score_shape, jnp.bfloat16),
                pltpu.VMEM(score_shape, jnp.bfloat16),
            ]
            + more_scratch,
        ),
        out_shape=out_shape,
        compiler_params=pltpu.CompilerParams(
            dimension_semantics=("arbitrary", "arbitrary"), vmem_limit_bytes=16 * 1024 * 1024
        ),
        cost_estimate=pl.CostEstimate(flops=10**10, bytes_accessed=4 * q.size, transcendentals=0),
        name="window_attention",
    )(docs, place, starts.reshape(1, total), *q_args, *g_args, *blocks)


def merge_kernel(place_ref, back_att, back_dq, att_in, dq_in, att_ref, dq_ref):
    att_ref[...] = back_att[...]
    dq_ref[...] = back_dq[...]


def merge(place, back, attended, query_grad, kv_heads):
    rows = back.shape[0]
    width = back.shape[1] // 2
    halves = [pl.BlockSpec((rows, width), lambda i, p, at=at: (0, at)) for at in range(2)]
    out = pl.BlockSpec((rows, width), lambda i, p: (0, 1 - p[1]))
    return pl.pallas_call(
        merge_kernel,
        grid_spec=pltpu.PrefetchScalarGridSpec(
            num_scalar_prefetch=1,
            grid=(1,),
            in_specs=halves + [pl.BlockSpec(memory_space=pl.ANY)] * 2,
            out_specs=[out, out],
        ),
        out_shape=[pltpu.HBM(attended.shape, attended.dtype)] * 2,
        input_output_aliases={3: 0, 4: 1},
        compiler_params=pltpu.CompilerParams(vmem_limit_bytes=8 * 1024 * 1024),
        cost_estimate=pl.CostEstimate(flops=0, bytes_accessed=8 * back.size, transcendentals=0),
        name="merge",
    )(place, back, back, attended, query_grad)


def on_device(queries, keys, values, doc_ids, output_gradient):
    n_ctx = lax.axis_size("ctx")
    parts = lax.axis_size("head")
    c = lax.axis_index("ctx")
    h = lax.axis_index("head")
    rows = queries.shape[0]
    width = keys.shape[1] // parts
    kv_heads = width // HEAD_SIZE
    fold = 2 if kv_heads == 2 and n_ctx % 2 == 0 and SPAN % 2 == 0 else 1
    side = lax.rem(c, fold)
    pair = 2 * HEAD_SIZE

    def turned(x, by):
        return lax.ppermute(x, "head", [(i, (i + by) % parts) for i in range(parts)])

    def shifted(x, by):
        return lax.ppermute(x, "ctx", [(i, i + by) for i in range(n_ctx) if 0 <= i + by < n_ctx])

    def swapped(x):
        return lax.ppermute(x, "ctx", [(i, i ^ 1) for i in range(n_ctx)])

    def columns(x, at, count):
        return lax.dynamic_slice_in_dim(x, at, count, 1)

    queries, output_gradient = (
        pltpu.with_memory_space_constraint(x, pltpu.HBM) for x in (queries, output_gradient)
    )
    pieces = []
    for r in range(parts):
        at = lax.rem(h + r, parts) * width
        piece = jnp.concatenate(
            [columns(x, at + n * HEAD_SIZE, HEAD_SIZE) for n in range(kv_heads) for x in (keys, values)], 1
        )
        pieces.append(turned(piece, r) if r else piece)

    q_other = g_other = None
    if fold > 1:
        q_other, g_other = (
            pltpu.with_memory_space_constraint(swapped(x), pltpu.VMEM) for x in (queries, output_gradient)
        )
    padded = jnp.concatenate([jnp.full((SPAN * rows,), -1, jnp.int32), doc_ids])
    docs = lax.dynamic_slice_in_dim(padded, (c - side) * rows, (SPAN + fold) * rows, 0)
    starts = jnp.sum((docs[:, None] < docs[None, :]).astype(jnp.int32), 0)
    place = jnp.stack([h, side]).astype(jnp.int32)

    own = jnp.concatenate(pieces, 0)
    if fold > 1:
        got = swapped(columns(own, (1 - side) * pair, pair))
        own = jnp.concatenate([columns(own, side * pair, pair), got], 0)
    backs = range(SPAN, 0, -fold)
    blocks = [shifted(own, back) for back in backs] + [own]

    results = attention(
        docs, starts, place, queries, output_gradient, q_other, g_other, blocks, parts, kv_heads, fold
    )
    grads = results[-len(blocks) :]
    total = grads[-1]
    for back, x in zip(backs, grads[:-1]):
        total = total + shifted(x, -back).astype(jnp.float32)
    total = total.astype(jnp.bfloat16)
    attended, query_grad = results[:2]
    if fold > 1:
        total = jnp.concatenate([total[:rows], swapped(total[rows:])], 1)
        attended, query_grad = merge(place, swapped(results[2]), attended, query_grad, kv_heads)

    small = rows // parts
    key_result = jnp.zeros(keys.shape, jnp.bfloat16)
    value_result = jnp.zeros(keys.shape, jnp.bfloat16)
    pieces = [total[r * small : (r + 1) * small] for r in range(parts)]
    pieces = [turned(piece, parts - r) if r else piece for r, piece in enumerate(pieces)]
    pieces, attended, query_grad = lax.optimization_barrier((pieces, attended, query_grad))
    for r, piece in enumerate(pieces):
        for n in range(kv_heads):
            head = jnp.bitwise_xor(side, n) if fold > 1 else n
            at = lax.rem(h + r, parts) * width + head * HEAD_SIZE
            low = n * pair
            mid, high = low + HEAD_SIZE, low + pair
            key_result = lax.dynamic_update_slice_in_dim(key_result, piece[:, low:mid], at, 1)
            value_result = lax.dynamic_update_slice_in_dim(value_result, piece[:, mid:high], at, 1)
    return (attended, query_grad, key_result, value_result)


def solution(mesh):
    in_specs = (
        P("ctx", "head"),
        P(("ctx", "head"), None),
        P(("ctx", "head"), None),
        P(),
        P("ctx", "head"),
    )
    out_specs = (
        P("ctx", "head"),
        P("ctx", "head"),
        P(("ctx", "head"), None),
        P(("ctx", "head"), None),
    )
    return jax.shard_map(
        on_device, mesh=mesh, in_specs=in_specs, out_specs=out_specs, check_vma=False
    )
```

profile of v0, /device:TPU:0, one launch (start us, length us, event | category | flops | bytes accessed | tf_op | source)
XLA Modules:
  0.0 56.5 jit_solution(16194635669571455429)
XLA Ops:
  0.7 0.0 copy-start.2
  0.7 1.0 %constant_dynamic-slice_fusion.16 = (bf16[64,128]{1,0:T(8,128)(2,1)S(1)}, bf16[64,128]{1,0:T(8,128)(2,1)S(1)}, bf16[64,128]{1,0:T(8,128)(2,1)S(1)}, bf16[64,128]...) fusion(bf16[64,1024]{1,0:T(8,128)(2,1)} %param.7, ...), kind=kLoop, calls=%fused_computation.50 | loop fusion | bytes 524320 | tf_op jit(solution)/shard_map/dynamic_slice | solution.py:284
  1.7 3.1 %collective-permute-start.2 = (bf16[64,512]{1,0:T(8,128)(2,1)S(1)}, bf16[64,512]{1,0:T(8,128)(2,1)S(1)}, u32[]{:S(2)}, u32[]{:S(2)}) collective-permute-start(bf16[64,512]{1,0:T(8,128)(2,1)S(1)} %pad_maximum_fusion.3), channel_id=1, source_target_pairs={{0,1},{1,2},{2,3},{3,0},{4,5},{5,6},{6,7},{7,4},{8,9},{9,10},{10,1... | collective-permute-start | bytes 196616 | tf_op jit(solution)/shard_map/ppermute | solution.py:275
  4.7 0.0 collective-permute-start
  4.8 0.5 collective-permute-start.1
  5.3 2.7 %collective-permute-start.3 = (bf16[64,512]{1,0:T(8,128)(2,1)S(1)}, bf16[64,512]{1,0:T(8,128)(2,1)S(1)}, u32[]{:S(2)}, u32[]{:S(2)}) collective-permute-start(bf16[64,512]{1,0:T(8,128)(2,1)S(1)} %pad_maximum_fusion.4), channel_id=1, source_target_pairs={{0,2},{1,3},{2,0},{3,1},{4,6},{5,7},{6,4},{7,5},{8,10},{9,11},{10,... | collective-permute-start | bytes 196616 | tf_op jit(solution)/shard_map/ppermute | solution.py:275
  7.9 1.4 %collective-permute-start.4 = (bf16[64,512]{1,0:T(8,128)(2,1)S(1)}, bf16[64,512]{1,0:T(8,128)(2,1)S(1)}, u32[]{:S(2)}, u32[]{:S(2)}) collective-permute-start(bf16[64,512]{1,0:T(8,128)(2,1)S(1)} %pad_maximum_fusion.5), channel_id=1, source_target_pairs={{0,3},{1,0},{2,1},{3,2},{4,7},{5,4},{6,5},{7,6},{8,11},{9,8},{10,9... | collective-permute-start | bytes 196616 | tf_op jit(solution)/shard_map/ppermute | solution.py:275
  9.3 0.0 collective-permute-done.2
  9.3 3.2 %collective-permute-done.3 = bf16[64,512]{1,0:T(8,128)(2,1)S(1)} collective-permute-done((bf16[64,512]{1,0:T(8,128)(2,1)S(1)}, bf16[64,512]{1,0:T(8,128)(2,1)S(1)}, u32[]{:S(2)}, u32[]{:S(2)}) %collective-permute-start.3) | collective-permute-done | bytes 65568 | tf_op jit(solution)/shard_map/ppermute | solution.py:275
  12.5 0.1 collective-permute-done.4
  12.6 0.1 collective-permute-start.5
  12.7 0.0 copy-done.2
  12.7 0.1 pad_dynamic-slice_fusion.refs_0_
  12.8 1.2 %collective-permute-done.5 = bf16[256,256]{1,0:T(8,128)(2,1)S(1)} collective-permute-done((bf16[256,256]{1,0:T(8,128)(2,1)S(1)}, bf16[256,256]{1,0:T(8,128)(2,1)S(1)}, u32[]{:S(2)}, u32[]{:S(2)}) %collective-permute-start.5) | collective-permute-done | bytes 131104 | tf_op jit(solution)/shard_map/ppermute | solution.py:281
  14.1 3.4 %collective-permute-start.6 = (bf16[512,256]{1,0:T(8,128)(2,1)S(1)}, bf16[512,256]{1,0:T(8,128)(2,1)S(1)}, u32[]{:S(2)}, u32[]{:S(2)}) collective-permute-start(bf16[512,256]{1,0:T(8,128)(2,1)S(1)} %pad_maximum_fusion.1.refs_8_), channel_id=1, source_target_pairs={{0,8},{4,12},{8,16},{12,20},{16,24},{20,28},{1,9},{5,13},{9,17},{1... | collective-permute-start | bytes 786440 | tf_op jit(solution)/shard_map/ppermute | solution.py:278
  17.5 0.1 pad_add_fusion.refs_1_.place_ref
  17.6 0.5 convert_reduce_fusion
  18.1 5.3 %collective-permute-done.6.refs_7_ = bf16[512,256]{1,0:T(8,128)(2,1)S(1)} collective-permute-done((bf16[512,256]{1,0:T(8,128)(2,1)S(1)}, bf16[512,256]{1,0:T(8,128)(2,1)S(1)}, u32[]{:S(2)}, u32[]{:S(2)}) %collective-permute-start.6) | collective-permute-done | bytes 262176 | tf_op jit(solution)/shard_map/ppermute | solution.py:278
  23.4 0.0 collective-permute-done.refs_4_
  23.4 0.0 collective-permute-done.1.refs_6_
  23.4 10.1 %window_attention.1 = (bf16[256,2048]{1,0:T(8,128)(2,1)}, bf16[256,2048]{1,0:T(8,128)(2,1)}, bf16[256,2048]{1,0:T(8,128)(2,1)}, bf16[512,256]{1,0:T(8,128)(2,1)S(1)}, f32[512,256]{1,0:T(8,128)S(1)}) custom-call(s32[1024]{0:T(1024)S(1)} %pad_dynamic-slice_fusion.refs_0_, s32[2]{0:T(128)S(1)} %pad_add_fusion.refs_1_.place_ref, s32[1,1024]{1,0:T(1,128)S(1)} %bitcast.3, ...), custom_call_target="tpu_custom_call" | custom-call | flops 10000000000 | bytes 2097152 | tf_op jit(solution)/shard_map/window_attention/pallas_call | solution.py:209
  33.5 1.3 %collective-permute-start.7 = (bf16[512,256]{1,0:T(8,128)(2,1)S(1)}, bf16[512,256]{1,0:T(8,128)(2,1)S(1)}, u32[]{:S(2)}, u32[]{:S(2)}) collective-permute-start(bf16[512,256]{1,0:T(8,128)(2,1)S(1)} %get-tuple-element.18), channel_id=1, source_target_pairs={{8,0},{12,4},{16,8},{20,12},{24,16},{28,20},{9,1},{13,5},{17,9},{2... | collective-permute-start | bytes 786440 | tf_op jit(solution)/shard_map/ppermute | solution.py:278
  34.8 0.1 collective-permute-start.12
  34.9 10.2 %collective-permute-done.7 = bf16[512,256]{1,0:T(8,128)(2,1)S(1)} collective-permute-done((bf16[512,256]{1,0:T(8,128)(2,1)S(1)}, bf16[512,256]{1,0:T(8,128)(2,1)S(1)}, u32[]{:S(2)}, u32[]{:S(2)}) %collective-permute-start.7) | collective-permute-done | bytes 262176 | tf_op jit(solution)/shard_map/ppermute | solution.py:278
  45.0 0.1 add_convert_fusion
  45.1 0.1 collective-permute-start.8
  45.2 1.3 %collective-permute-done.8 = bf16[256,256]{1,0:T(8,128)(2,1)S(1)} collective-permute-done((bf16[256,256]{1,0:T(8,128)(2,1)S(1)}, bf16[256,256]{1,0:T(8,128)(2,1)S(1)}, u32[]{:S(2)}, u32[]{:S(2)}) %collective-permute-start.8) | collective-permute-done | bytes 131104 | tf_op jit(solution)/shard_map/ppermute | solution.py:281
  46.6 1.1 %collective-permute-start.10 = (bf16[64,512]{1,0:T(8,128)(2,1)S(1)}, bf16[64,512]{1,0:T(8,128)(2,1)S(1)}, u32[]{:S(2)}, u32[]{:S(2)}) collective-permute-start(bf16[64,512]{1,0:T(8,128)(2,1)S(1)} %get-tuple-element.33), channel_id=1, source_target_pairs={{0,2},{1,3},{2,0},{3,1},{4,6},{5,7},{6,4},{7,5},{8,10},{9,11},{10,... | collective-permute-start | bytes 196616 | tf_op jit(solution)/shard_map/ppermute | solution.py:275
  47.6 2.5 %collective-permute-start.11 = (bf16[64,512]{1,0:T(8,128)(2,1)S(1)}, bf16[64,512]{1,0:T(8,128)(2,1)S(1)}, u32[]{:S(2)}, u32[]{:S(2)}) collective-permute-start(bf16[64,512]{1,0:T(8,128)(2,1)S(1)} %get-tuple-element.30), channel_id=1, source_target_pairs={{0,1},{1,2},{2,3},{3,0},{4,5},{5,6},{6,7},{7,4},{8,9},{9,10},{10,1... | collective-permute-start | bytes 196616 | tf_op jit(solution)/shard_map/ppermute | solution.py:275
  50.1 1.3 %collective-permute-start.9 = (bf16[64,512]{1,0:T(8,128)(2,1)S(1)}, bf16[64,512]{1,0:T(8,128)(2,1)S(1)}, u32[]{:S(2)}, u32[]{:S(2)}) collective-permute-start(bf16[64,512]{1,0:T(8,128)(2,1)S(1)} %get-tuple-element.32), channel_id=1, source_target_pairs={{0,3},{1,0},{2,1},{3,2},{4,7},{5,4},{6,5},{7,6},{8,11},{9,8},{10,9... | collective-permute-start | bytes 196616 | tf_op jit(solution)/shard_map/ppermute | solution.py:275
  51.5 0.0 collective-permute-done.12.back_att.back_dq
  51.5 1.6 %merge.1 = (bf16[256,2048]{1,0:T(8,128)(2,1)}, bf16[256,2048]{1,0:T(8,128)(2,1)}) custom-call(s32[2]{0:T(128)S(1)} %pad_add_fusion.refs_1_.place_ref, bf16[256,2048]{1,0:T(8,128)(2,1)S(1)} %collective-permute-done.12.back_att.back_dq, bf16[256,2048]{1,0:T(8,128)(2,1)S(1)} %collective-permute-done.12.back_att.back_dq, ...), custom_call_target="tpu_custom_call", output_to_operand_aliasing={{0}: (3, {}), {1}: (4, {})} | custom-call | bytes 4194304 | tf_op jit(solution)/shard_map/merge/pallas_call | solution.py:246
  53.0 2.1 %collective-permute-done.10 = bf16[64,512]{1,0:T(8,128)(2,1)S(1)} collective-permute-done((bf16[64,512]{1,0:T(8,128)(2,1)S(1)}, bf16[64,512]{1,0:T(8,128)(2,1)S(1)}, u32[]{:S(2)}, u32[]{:S(2)}) %collective-permute-start.10) | collective-permute-done | bytes 65568 | tf_op jit(solution)/shard_map/ppermute | solution.py:275
  55.2 0.0 collective-permute-done.11
  55.2 0.3 collective-permute-done.9
  55.8 0.0 copy-start.1
  55.8 0.0 copy-start
  55.8 0.6 %copy-done.1 = bf16[64,1024]{1,0:T(8,128)(2,1)} copy-done((bf16[64,1024]{1,0:T(8,128)(2,1)}, bf16[64,1024]{1,0:T(8,128)(2,1)S(1)}, u32[]{:S(2)}) %copy-start.1) | copy-done | bytes 131096
  56.4 0.0 copy-done
  (22 shorter events, 0.4 us)
Async XLA Ops:
  0.7 12.1 %copy-start.2 = (s32[2048]{0:T(1024)S(1)}, s32[2048]{0:T(1024)}, u32[]{:S(2)}) copy-start(s32[2048]{0:T(1024)} %param.8) | copy-start | bytes 24580
  1.7 7.7 %collective-permute-start.2 = (bf16[64,512]{1,0:T(8,128)(2,1)S(1)}, bf16[64,512]{1,0:T(8,128)(2,1)S(1)}, u32[]{:S(2)}, u32[]{:S(2)}) collective-permute-start(bf16[64,512]{1,0:T(8,128)(2,1)S(1)} %pad_maximum_fusion.3), channel_id=1, source_target_pairs={{0,1},{1,2},{2,3},{3,0},{4,5},{5,6},{6,7},{7,4},{8,9},{9,10},{10,1... | collective-permute-start | bytes 196616 | tf_op jit(solution)/shard_map/ppermute | solution.py:275
  4.7 18.6 %collective-permute-start = (bf16[256,2048]{1,0:T(8,128)(2,1)}, bf16[256,2048]{1,0:T(8,128)(2,1)S(1)}, u32[]{:S(2)}, u32[]{:S(2)}) collective-permute-start(bf16[256,2048]{1,0:T(8,128)(2,1)} %refs_3_.1), channel_id=1, source_target_pairs={{0,4},{4,0},{8,12},{12,8},{16,20},{20,16},{24,28},{28,24},{1,5},{5... | collective-permute-start | bytes 3145736 | tf_op jit(solution)/shard_map/ppermute | solution.py:281
  4.8 18.6 %collective-permute-start.1 = (bf16[256,2048]{1,0:T(8,128)(2,1)}, bf16[256,2048]{1,0:T(8,128)(2,1)S(1)}, u32[]{:S(2)}, u32[]{:S(2)}) collective-permute-start(bf16[256,2048]{1,0:T(8,128)(2,1)} %refs_5_.1), channel_id=1, source_target_pairs={{0,4},{4,0},{8,12},{12,8},{16,20},{20,16},{24,28},{28,24},{1,5},{5... | collective-permute-start | bytes 3145736 | tf_op jit(solution)/shard_map/ppermute | solution.py:281
  5.3 7.2 %collective-permute-start.3 = (bf16[64,512]{1,0:T(8,128)(2,1)S(1)}, bf16[64,512]{1,0:T(8,128)(2,1)S(1)}, u32[]{:S(2)}, u32[]{:S(2)}) collective-permute-start(bf16[64,512]{1,0:T(8,128)(2,1)S(1)} %pad_maximum_fusion.4), channel_id=1, source_target_pairs={{0,2},{1,3},{2,0},{3,1},{4,6},{5,7},{6,4},{7,5},{8,10},{9,11},{10,... | collective-permute-start | bytes 196616 | tf_op jit(solution)/shard_map/ppermute | solution.py:275
  7.9 4.6 %collective-permute-start.4 = (bf16[64,512]{1,0:T(8,128)(2,1)S(1)}, bf16[64,512]{1,0:T(8,128)(2,1)S(1)}, u32[]{:S(2)}, u32[]{:S(2)}) collective-permute-start(bf16[64,512]{1,0:T(8,128)(2,1)S(1)} %pad_maximum_fusion.5), channel_id=1, source_target_pairs={{0,3},{1,0},{2,1},{3,2},{4,7},{5,4},{6,5},{7,6},{8,11},{9,8},{10,9... | collective-permute-start | bytes 196616 | tf_op jit(solution)/shard_map/ppermute | solution.py:275
  12.6 1.4 %collective-permute-start.5 = (bf16[256,256]{1,0:T(8,128)(2,1)S(1)}, bf16[256,256]{1,0:T(8,128)(2,1)S(1)}, u32[]{:S(2)}, u32[]{:S(2)}) collective-permute-start(bf16[256,256]{1,0:T(8,128)(2,1)S(1)} %get-tuple-element.37), channel_id=1, source_target_pairs={{0,4},{4,0},{8,12},{12,8},{16,20},{20,16},{24,28},{28,24},{1,5},{5... | collective-permute-start | bytes 393224 | tf_op jit(solution)/shard_map/ppermute | solution.py:281
  14.1 9.3 %collective-permute-start.6 = (bf16[512,256]{1,0:T(8,128)(2,1)S(1)}, bf16[512,256]{1,0:T(8,128)(2,1)S(1)}, u32[]{:S(2)}, u32[]{:S(2)}) collective-permute-start(bf16[512,256]{1,0:T(8,128)(2,1)S(1)} %pad_maximum_fusion.1.refs_8_), channel_id=1, source_target_pairs={{0,8},{4,12},{8,16},{12,20},{16,24},{20,28},{1,9},{5,13},{9,17},{1... | collective-permute-start | bytes 786440 | tf_op jit(solution)/shard_map/ppermute | solution.py:278
  33.5 11.5 %collective-permute-start.7 = (bf16[512,256]{1,0:T(8,128)(2,1)S(1)}, bf16[512,256]{1,0:T(8,128)(2,1)S(1)}, u32[]{:S(2)}, u32[]{:S(2)}) collective-permute-start(bf16[512,256]{1,0:T(8,128)(2,1)S(1)} %get-tuple-element.18), channel_id=1, source_target_pairs={{8,0},{12,4},{16,8},{20,12},{24,16},{28,20},{9,1},{13,5},{17,9},{2... | collective-permute-start | bytes 786440 | tf_op jit(solution)/shard_map/ppermute | solution.py:278
  34.8 16.7 %collective-permute-start.12 = (bf16[256,2048]{1,0:T(8,128)(2,1)}, bf16[256,2048]{1,0:T(8,128)(2,1)S(1)}, u32[]{:S(2)}, u32[]{:S(2)}) collective-permute-start(bf16[256,2048]{1,0:T(8,128)(2,1)} %get-tuple-element.19), channel_id=1, source_target_pairs={{0,4},{4,0},{8,12},{12,8},{16,20},{20,16},{24,28},{28,24},{1,5},{5... | collective-permute-start | bytes 3145736 | tf_op jit(solution)/shard_map/ppermute | solution.py:281
  45.1 1.4 %collective-permute-start.8 = (bf16[256,256]{1,0:T(8,128)(2,1)S(1)}, bf16[256,256]{1,0:T(8,128)(2,1)S(1)}, u32[]{:S(2)}, u32[]{:S(2)}) collective-permute-start(bf16[256,256]{1,0:T(8,128)(2,1)S(1)} %get-tuple-element.34), channel_id=1, source_target_pairs={{0,4},{4,0},{8,12},{12,8},{16,20},{20,16},{24,28},{28,24},{1,5},{5... | collective-permute-start | bytes 393224 | tf_op jit(solution)/shard_map/ppermute | solution.py:281
  46.6 8.6 %collective-permute-start.10 = (bf16[64,512]{1,0:T(8,128)(2,1)S(1)}, bf16[64,512]{1,0:T(8,128)(2,1)S(1)}, u32[]{:S(2)}, u32[]{:S(2)}) collective-permute-start(bf16[64,512]{1,0:T(8,128)(2,1)S(1)} %get-tuple-element.33), channel_id=1, source_target_pairs={{0,2},{1,3},{2,0},{3,1},{4,6},{5,7},{6,4},{7,5},{8,10},{9,11},{10,... | collective-permute-start | bytes 196616 | tf_op jit(solution)/shard_map/ppermute | solution.py:275
  47.6 7.5 %collective-permute-start.11 = (bf16[64,512]{1,0:T(8,128)(2,1)S(1)}, bf16[64,512]{1,0:T(8,128)(2,1)S(1)}, u32[]{:S(2)}, u32[]{:S(2)}) collective-permute-start(bf16[64,512]{1,0:T(8,128)(2,1)S(1)} %get-tuple-element.30), channel_id=1, source_target_pairs={{0,1},{1,2},{2,3},{3,0},{4,5},{5,6},{6,7},{7,4},{8,9},{9,10},{10,1... | collective-permute-start | bytes 196616 | tf_op jit(solution)/shard_map/ppermute | solution.py:275
  50.1 5.4 %collective-permute-start.9 = (bf16[64,512]{1,0:T(8,128)(2,1)S(1)}, bf16[64,512]{1,0:T(8,128)(2,1)S(1)}, u32[]{:S(2)}, u32[]{:S(2)}) collective-permute-start(bf16[64,512]{1,0:T(8,128)(2,1)S(1)} %get-tuple-element.32), channel_id=1, source_target_pairs={{0,3},{1,0},{2,1},{3,2},{4,7},{5,4},{6,5},{7,6},{8,11},{9,8},{10,9... | collective-permute-start | bytes 196616 | tf_op jit(solution)/shard_map/ppermute | solution.py:275
  55.8 0.7 %copy-start.1 = (bf16[64,1024]{1,0:T(8,128)(2,1)}, bf16[64,1024]{1,0:T(8,128)(2,1)S(1)}, u32[]{:S(2)}) copy-start(bf16[64,1024]{1,0:T(8,128)(2,1)S(1)} %get-tuple-element.54) | copy-start | bytes 393220
  55.8 0.7 %copy-start = (bf16[64,1024]{1,0:T(8,128)(2,1)}, bf16[64,1024]{1,0:T(8,128)(2,1)S(1)}, u32[]{:S(2)}) copy-start(bf16[64,1024]{1,0:T(8,128)(2,1)S(1)} %slice_dynamic-update-slice_fusion.8) | copy-start | bytes 393220
where the time goes:
time: 56.7 us; the launch traced here: 56.5 us
  waiting for transfers between devices  23.7 us (42%)
  starting transfers between devices  17.5 us (31%)
  Pallas kernels  11.7 us (21%)
  local copies, waits for them, and re-layouts  1.98 us (3%)
  between operations  0.9 us (2%)
  other arithmetic  0.7 us (1%)
    ppermute x2, waiting for transfers between devices, shifted(): lax.ppermute(x, 'ctx', [(i, i + by) for i in range(n_ctx) if 0 <= i + by...  15.5 us
    ppermute x6, starting transfers between devices, turned(): lax.ppermute(x, 'head', [(i, (i + by) % parts) for i in range(parts)])  12 us
    pallas_call x1, Pallas kernels, attention(): pl.pallas_call(functools.partial(window_kernel, parts=parts, groups=group...  10.1 us
    ppermute x6, waiting for transfers between devices, turned(): lax.ppermute(x, 'head', [(i, (i + by) % parts) for i in range(parts)])  5.68 us
    ppermute x2, starting transfers between devices, shifted(): lax.ppermute(x, 'ctx', [(i, i + by) for i in range(n_ctx) if 0 <= i + by...  4.73 us
    ppermute x5, waiting for transfers between devices, swapped(): return lax.ppermute(x, 'ctx', [(i, i ^ 1) for i in range(n_ctx)])  2.58 us
    pallas_call x1, Pallas kernels, merge(): pl.pallas_call(merge_kernel, grid_spec=pltpu.PrefetchScalarGridSpec(num_s...  1.57 us
  transfers between devices with their start and end apart: 13, of which 8 were waited for; matrix products, arithmetic and copies ran while one was open for 1% of the time, Pallas kernels for 3%

commit v1 on v0

--- a/solution.py
+++ b/solution.py
@@ -133,15 +133,16 @@
 
         def differ(c):
             dp = lax.dot_general(vw[window, :], rows_of(g_ref, c), LAST, preferred_element_type=jnp.float32)
+            scaled = inverses[c] * score_scale
             for b in range(tiles):
-                p = s_sc[c, tile(b), :] * inverses[c]
+                p = s_sc[c, tile(b), :] * scaled
                 ds_sc[c, tile(b), :] = (p * (dp[tile(b)] - deltas[c])).astype(jnp.bfloat16)
 
         def spread(c):
             w = w_sc[c, : tiles * TILE, :]
             ds = ds_sc[c, : tiles * TILE, :]
             dq = lax.dot_general(ds, kw[window, :], FIRST, preferred_element_type=jnp.float32)
-            dq = (dq * score_scale).astype(jnp.bfloat16)
+            dq = dq.astype(jnp.bfloat16)
             for j in range(2):
                 dq_sc[:, (2 * c + j) * HEAD_SIZE : (2 * c + j + 1) * HEAD_SIZE] = dq[tile(j)]
             dv_acc[window, :] += jnp.dot(w, rows_of(g_ref, c), preferred_element_type=jnp.float32)
@@ -175,7 +176,7 @@
     def _():
         for b, ref in enumerate(block_grads):
             for here, token in places(b):
-                ref[here, :HEAD_SIZE] = (dk_acc[token, :] * score_scale).astype(ref.dtype)
+                ref[here, :HEAD_SIZE] = dk_acc[token, :].astype(ref.dtype)
                 ref[here, HEAD_SIZE:] = dv_acc[token, :].astype(ref.dtype)
 
 
@@ -275,7 +276,7 @@
         return lax.ppermute(x, "head", [(i, (i + by) % parts) for i in range(parts)])
 
     def shifted(x, by):
-        return lax.ppermute(x, "ctx", [(i, i + by) for i in range(n_ctx) if 0 <= i + by < n_ctx])
+        return lax.ppermute(x, "ctx", [(i, (i + by) % n_ctx) for i in range(n_ctx)])
 
     def swapped(x):
         return lax.ppermute(x, "ctx", [(i, i ^ 1) for i in range(n_ctx)])

time: 56.7 us -> 54.6 us (0.963)
  waiting for transfers between devices: 23.7 us -> 20.5 us
  starting transfers between devices: 17.5 us -> 19.2 us
    ppermute x2, waiting for transfers between devices: 15.5 us -> 12.2 us  [shifted(): return lax.ppermute(x, 'ctx', [(i, (i + by) % n_ctx) for i in range(n_ctx)])]
    ppermute x2, starting transfers between devices: 4.73 us -> 6.48 us  [shifted(): return lax.ppermute(x, 'ctx', [(i, (i + by) % n_ctx) for i in range(n_ctx)])]
where the time goes in v1:
time: 54.6 us; the launch traced here: 54.5 us
  waiting for transfers between devices  20.5 us (38%)
  starting transfers between devices  19.2 us (35%)
  Pallas kernels  11.3 us (21%)
  local copies, waits for them, and re-layouts  1.98 us (4%)
  between operations  0.88 us (2%)
  other arithmetic  0.7 us (1%)
    ppermute x2, waiting for transfers between devices, shifted(): return lax.ppermute(x, 'ctx', [(i, (i + by) % n_ctx) for i in range(n_ctx)])  12.2 us
    ppermute x6, starting transfers between devices, turned(): lax.ppermute(x, 'head', [(i, (i + by) % parts) for i in range(parts)])  12 us
    pallas_call x1, Pallas kernels, attention(): pl.pallas_call(functools.partial(window_kernel, parts=parts, groups=group...  9.73 us
    ppermute x2, starting transfers between devices, shifted(): return lax.ppermute(x, 'ctx', [(i, (i + by) % n_ctx) for i in range(n_ctx)])  6.48 us
    ppermute x6, waiting for transfers between devices, turned(): lax.ppermute(x, 'head', [(i, (i + by) % parts) for i in range(parts)])  5.68 us
    ppermute x5, waiting for transfers between devices, swapped(): return lax.ppermute(x, 'ctx', [(i, i ^ 1) for i in range(n_ctx)])  2.58 us
    pallas_call x1, Pallas kernels, merge(): pl.pallas_call(merge_kernel, grid_spec=pltpu.PrefetchScalarGridSpec(num_s...  1.57 us
  transfers between devices with their start and end apart: 13, of which 8 were waited for; matrix products, arithmetic and copies ran while one was open for 1% of the time, Pallas kernels for 3%

profile of v1, /device:TPU:0, one launch (start us, length us, event | category | flops | bytes accessed | tf_op | source)
XLA Modules:
  0.0 54.5 jit_solution(14312135585900369640)
XLA Ops:
  0.7 0.0 copy-start.2
  0.7 1.0 %constant_dynamic-slice_fusion.16 = (bf16[64,128]{1,0:T(8,128)(2,1)S(1)}, bf16[64,128]{1,0:T(8,128)(2,1)S(1)}, bf16[64,128]{1,0:T(8,128)(2,1)S(1)}, bf16[64,128]...) fusion(bf16[64,1024]{1,0:T(8,128)(2,1)} %param.7, ...), kind=kLoop, calls=%fused_computation.50 | loop fusion | bytes 524320 | tf_op jit(solution)/shard_map/dynamic_slice | solution.py:285
  1.7 3.1 %collective-permute-start.2 = (bf16[64,512]{1,0:T(8,128)(2,1)S(1)}, bf16[64,512]{1,0:T(8,128)(2,1)S(1)}, u32[]{:S(2)}, u32[]{:S(2)}) collective-permute-start(bf16[64,512]{1,0:T(8,128)(2,1)S(1)} %pad_maximum_fusion.3), channel_id=1, source_target_pairs={{0,1},{1,2},{2,3},{3,0},{4,5},{5,6},{6,7},{7,4},{8,9},{9,10},{10,1... | collective-permute-start | bytes 196616 | tf_op jit(solution)/shard_map/ppermute | solution.py:276
  4.7 0.0 collective-permute-start
  4.8 0.5 collective-permute-start.1
  5.3 2.7 %collective-permute-start.3 = (bf16[64,512]{1,0:T(8,128)(2,1)S(1)}, bf16[64,512]{1,0:T(8,128)(2,1)S(1)}, u32[]{:S(2)}, u32[]{:S(2)}) collective-permute-start(bf16[64,512]{1,0:T(8,128)(2,1)S(1)} %pad_maximum_fusion.4), channel_id=1, source_target_pairs={{0,2},{1,3},{2,0},{3,1},{4,6},{5,7},{6,4},{7,5},{8,10},{9,11},{10,... | collective-permute-start | bytes 196616 | tf_op jit(solution)/shard_map/ppermute | solution.py:276
  7.9 1.4 %collective-permute-start.4 = (bf16[64,512]{1,0:T(8,128)(2,1)S(1)}, bf16[64,512]{1,0:T(8,128)(2,1)S(1)}, u32[]{:S(2)}, u32[]{:S(2)}) collective-permute-start(bf16[64,512]{1,0:T(8,128)(2,1)S(1)} %pad_maximum_fusion.5), channel_id=1, source_target_pairs={{0,3},{1,0},{2,1},{3,2},{4,7},{5,4},{6,5},{7,6},{8,11},{9,8},{10,9... | collective-permute-start | bytes 196616 | tf_op jit(solution)/shard_map/ppermute | solution.py:276
  9.3 0.0 collective-permute-done.2
  9.3 3.2 %collective-permute-done.3 = bf16[64,512]{1,0:T(8,128)(2,1)S(1)} collective-permute-done((bf16[64,512]{1,0:T(8,128)(2,1)S(1)}, bf16[64,512]{1,0:T(8,128)(2,1)S(1)}, u32[]{:S(2)}, u32[]{:S(2)}) %collective-permute-start.3) | collective-permute-done | bytes 65568 | tf_op jit(solution)/shard_map/ppermute | solution.py:276
  12.5 0.1 collective-permute-done.4
  12.6 0.1 collective-permute-start.5
  12.7 0.0 copy-done.2
  12.7 0.1 pad_dynamic-slice_fusion.refs_0_
  12.8 1.2 %collective-permute-done.5 = bf16[256,256]{1,0:T(8,128)(2,1)S(1)} collective-permute-done((bf16[256,256]{1,0:T(8,128)(2,1)S(1)}, bf16[256,256]{1,0:T(8,128)(2,1)S(1)}, u32[]{:S(2)}, u32[]{:S(2)}) %collective-permute-start.5) | collective-permute-done | bytes 131104 | tf_op jit(solution)/shard_map/ppermute | solution.py:282
  14.1 1.6 %collective-permute-start.6 = (bf16[512,256]{1,0:T(8,128)(2,1)S(1)}, bf16[512,256]{1,0:T(8,128)(2,1)S(1)}, u32[]{:S(2)}, u32[]{:S(2)}) collective-permute-start(bf16[512,256]{1,0:T(8,128)(2,1)S(1)} %pad_maximum_fusion.1.refs_8_), channel_id=1, source_target_pairs={{0,8},{4,12},{8,16},{12,20},{16,24},{20,28},{24,0},{28,4},{1,9},{5... | collective-permute-start | bytes 786440 | tf_op jit(solution)/shard_map/ppermute | solution.py:279
  15.7 0.1 pad_add_fusion.refs_1_.place_ref
  15.7 0.5 convert_reduce_fusion
  16.2 7.2 %collective-permute-done.6.refs_7_ = bf16[512,256]{1,0:T(8,128)(2,1)S(1)} collective-permute-done((bf16[512,256]{1,0:T(8,128)(2,1)S(1)}, bf16[512,256]{1,0:T(8,128)(2,1)S(1)}, u32[]{:S(2)}, u32[]{:S(2)}) %collective-permute-start.6) | collective-permute-done | bytes 262176 | tf_op jit(solution)/shard_map/ppermute | solution.py:279
  23.4 0.0 collective-permute-done.refs_4_
  23.4 0.0 collective-permute-done.1.refs_6_
  23.4 9.7 %window_attention.1 = (bf16[256,2048]{1,0:T(8,128)(2,1)}, bf16[256,2048]{1,0:T(8,128)(2,1)}, bf16[256,2048]{1,0:T(8,128)(2,1)}, bf16[512,256]{1,0:T(8,128)(2,1)S(1)}, f32[512,256]{1,0:T(8,128)S(1)}) custom-call(s32[1024]{0:T(1024)S(1)} %pad_dynamic-slice_fusion.refs_0_, s32[2]{0:T(128)S(1)} %pad_add_fusion.refs_1_.place_ref, s32[1,1024]{1,0:T(1,128)S(1)} %bitcast.3, ...), custom_call_target="tpu_custom_call" | custom-call | flops 10000000000 | bytes 2097152 | tf_op jit(solution)/shard_map/window_attention/pallas_call | solution.py:210
  33.1 4.9 %collective-permute-start.7 = (bf16[512,256]{1,0:T(8,128)(2,1)S(1)}, bf16[512,256]{1,0:T(8,128)(2,1)S(1)}, u32[]{:S(2)}, u32[]{:S(2)}) collective-permute-start(bf16[512,256]{1,0:T(8,128)(2,1)S(1)} %get-tuple-element.18), channel_id=1, source_target_pairs={{0,24},{4,28},{8,0},{12,4},{16,8},{20,12},{24,16},{28,20},{1,25},{... | collective-permute-start | bytes 786440 | tf_op jit(solution)/shard_map/ppermute | solution.py:279
  38.0 0.0 collective-permute-start.12
  38.0 5.1 %collective-permute-done.7 = bf16[512,256]{1,0:T(8,128)(2,1)S(1)} collective-permute-done((bf16[512,256]{1,0:T(8,128)(2,1)S(1)}, bf16[512,256]{1,0:T(8,128)(2,1)S(1)}, u32[]{:S(2)}, u32[]{:S(2)}) %collective-permute-start.7) | collective-permute-done | bytes 262176 | tf_op jit(solution)/shard_map/ppermute | solution.py:279
  43.1 0.1 add_convert_fusion
  43.2 0.1 collective-permute-start.8
  43.2 1.3 %collective-permute-done.8 = bf16[256,256]{1,0:T(8,128)(2,1)S(1)} collective-permute-done((bf16[256,256]{1,0:T(8,128)(2,1)S(1)}, bf16[256,256]{1,0:T(8,128)(2,1)S(1)}, u32[]{:S(2)}, u32[]{:S(2)}) %collective-permute-start.8) | collective-permute-done | bytes 131104 | tf_op jit(solution)/shard_map/ppermute | solution.py:282
  44.6 1.1 %collective-permute-start.10 = (bf16[64,512]{1,0:T(8,128)(2,1)S(1)}, bf16[64,512]{1,0:T(8,128)(2,1)S(1)}, u32[]{:S(2)}, u32[]{:S(2)}) collective-permute-start(bf16[64,512]{1,0:T(8,128)(2,1)S(1)} %get-tuple-element.33), channel_id=1, source_target_pairs={{0,2},{1,3},{2,0},{3,1},{4,6},{5,7},{6,4},{7,5},{8,10},{9,11},{10,... | collective-permute-start | bytes 196616 | tf_op jit(solution)/shard_map/ppermute | solution.py:276
  45.7 2.5 %collective-permute-start.11 = (bf16[64,512]{1,0:T(8,128)(2,1)S(1)}, bf16[64,512]{1,0:T(8,128)(2,1)S(1)}, u32[]{:S(2)}, u32[]{:S(2)}) collective-permute-start(bf16[64,512]{1,0:T(8,128)(2,1)S(1)} %get-tuple-element.30), channel_id=1, source_target_pairs={{0,1},{1,2},{2,3},{3,0},{4,5},{5,6},{6,7},{7,4},{8,9},{9,10},{10,1... | collective-permute-start | bytes 196616 | tf_op jit(solution)/shard_map/ppermute | solution.py:276
  48.2 1.3 %collective-permute-start.9 = (bf16[64,512]{1,0:T(8,128)(2,1)S(1)}, bf16[64,512]{1,0:T(8,128)(2,1)S(1)}, u32[]{:S(2)}, u32[]{:S(2)}) collective-permute-start(bf16[64,512]{1,0:T(8,128)(2,1)S(1)} %get-tuple-element.32), channel_id=1, source_target_pairs={{0,3},{1,0},{2,1},{3,2},{4,7},{5,4},{6,5},{7,6},{8,11},{9,8},{10,9... | collective-permute-start | bytes 196616 | tf_op jit(solution)/shard_map/ppermute | solution.py:276
  49.5 0.0 collective-permute-done.12.back_att.back_dq
  49.5 1.6 %merge.1 = (bf16[256,2048]{1,0:T(8,128)(2,1)}, bf16[256,2048]{1,0:T(8,128)(2,1)}) custom-call(s32[2]{0:T(128)S(1)} %pad_add_fusion.refs_1_.place_ref, bf16[256,2048]{1,0:T(8,128)(2,1)S(1)} %collective-permute-done.12.back_att.back_dq, bf16[256,2048]{1,0:T(8,128)(2,1)S(1)} %collective-permute-done.12.back_att.back_dq, ...), custom_call_target="tpu_custom_call", output_to_operand_aliasing={{0}: (3, {}), {1}: (4, {})} | custom-call | bytes 4194304 | tf_op jit(solution)/shard_map/merge/pallas_call | solution.py:247
  51.1 2.1 %collective-permute-done.10 = bf16[64,512]{1,0:T(8,128)(2,1)S(1)} collective-permute-done((bf16[64,512]{1,0:T(8,128)(2,1)S(1)}, bf16[64,512]{1,0:T(8,128)(2,1)S(1)}, u32[]{:S(2)}, u32[]{:S(2)}) %collective-permute-start.10) | collective-permute-done | bytes 65568 | tf_op jit(solution)/shard_map/ppermute | solution.py:276
  53.2 0.0 collective-permute-done.11
  53.2 0.3 collective-permute-done.9
  53.8 0.0 copy-start.1
  53.8 0.0 copy-start
  53.9 0.6 %copy-done.1 = bf16[64,1024]{1,0:T(8,128)(2,1)} copy-done((bf16[64,1024]{1,0:T(8,128)(2,1)}, bf16[64,1024]{1,0:T(8,128)(2,1)S(1)}, u32[]{:S(2)}) %copy-start.1) | copy-done | bytes 131096
  54.5 0.0 copy-done
  (22 shorter events, 0.4 us)
Async XLA Ops:
  0.7 12.1 %copy-start.2 = (s32[2048]{0:T(1024)S(1)}, s32[2048]{0:T(1024)}, u32[]{:S(2)}) copy-start(s32[2048]{0:T(1024)} %param.8) | copy-start | bytes 24580
  1.7 7.7 %collective-permute-start.2 = (bf16[64,512]{1,0:T(8,128)(2,1)S(1)}, bf16[64,512]{1,0:T(8,128)(2,1)S(1)}, u32[]{:S(2)}, u32[]{:S(2)}) collective-permute-start(bf16[64,512]{1,0:T(8,128)(2,1)S(1)} %pad_maximum_fusion.3), channel_id=1, source_target_pairs={{0,1},{1,2},{2,3},{3,0},{4,5},{5,6},{6,7},{7,4},{8,9},{9,10},{10,1... | collective-permute-start | bytes 196616 | tf_op jit(solution)/shard_map/ppermute | solution.py:276
  4.7 18.6 %collective-permute-start = (bf16[256,2048]{1,0:T(8,128)(2,1)}, bf16[256,2048]{1,0:T(8,128)(2,1)S(1)}, u32[]{:S(2)}, u32[]{:S(2)}) collective-permute-start(bf16[256,2048]{1,0:T(8,128)(2,1)} %refs_3_.1), channel_id=1, source_target_pairs={{0,4},{4,0},{8,12},{12,8},{16,20},{20,16},{24,28},{28,24},{1,5},{5... | collective-permute-start | bytes 3145736 | tf_op jit(solution)/shard_map/ppermute | solution.py:282
  4.8 18.6 %collective-permute-start.1 = (bf16[256,2048]{1,0:T(8,128)(2,1)}, bf16[256,2048]{1,0:T(8,128)(2,1)S(1)}, u32[]{:S(2)}, u32[]{:S(2)}) collective-permute-start(bf16[256,2048]{1,0:T(8,128)(2,1)} %refs_5_.1), channel_id=1, source_target_pairs={{0,4},{4,0},{8,12},{12,8},{16,20},{20,16},{24,28},{28,24},{1,5},{5... | collective-permute-start | bytes 3145736 | tf_op jit(solution)/shard_map/ppermute | solution.py:282
  5.3 7.2 %collective-permute-start.3 = (bf16[64,512]{1,0:T(8,128)(2,1)S(1)}, bf16[64,512]{1,0:T(8,128)(2,1)S(1)}, u32[]{:S(2)}, u32[]{:S(2)}) collective-permute-start(bf16[64,512]{1,0:T(8,128)(2,1)S(1)} %pad_maximum_fusion.4), channel_id=1, source_target_pairs={{0,2},{1,3},{2,0},{3,1},{4,6},{5,7},{6,4},{7,5},{8,10},{9,11},{10,... | collective-permute-start | bytes 196616 | tf_op jit(solution)/shard_map/ppermute | solution.py:276
  7.9 4.6 %collective-permute-start.4 = (bf16[64,512]{1,0:T(8,128)(2,1)S(1)}, bf16[64,512]{1,0:T(8,128)(2,1)S(1)}, u32[]{:S(2)}, u32[]{:S(2)}) collective-permute-start(bf16[64,512]{1,0:T(8,128)(2,1)S(1)} %pad_maximum_fusion.5), channel_id=1, source_target_pairs={{0,3},{1,0},{2,1},{3,2},{4,7},{5,4},{6,5},{7,6},{8,11},{9,8},{10,9... | collective-permute-start | bytes 196616 | tf_op jit(solution)/shard_map/ppermute | solution.py:276
  12.6 1.4 %collective-permute-start.5 = (bf16[256,256]{1,0:T(8,128)(2,1)S(1)}, bf16[256,256]{1,0:T(8,128)(2,1)S(1)}, u32[]{:S(2)}, u32[]{:S(2)}) collective-permute-start(bf16[256,256]{1,0:T(8,128)(2,1)S(1)} %get-tuple-element.37), channel_id=1, source_target_pairs={{0,4},{4,0},{8,12},{12,8},{16,20},{20,16},{24,28},{28,24},{1,5},{5... | collective-permute-start | bytes 393224 | tf_op jit(solution)/shard_map/ppermute | solution.py:282
  14.1 9.3 %collective-permute-start.6 = (bf16[512,256]{1,0:T(8,128)(2,1)S(1)}, bf16[512,256]{1,0:T(8,128)(2,1)S(1)}, u32[]{:S(2)}, u32[]{:S(2)}) collective-permute-start(bf16[512,256]{1,0:T(8,128)(2,1)S(1)} %pad_maximum_fusion.1.refs_8_), channel_id=1, source_target_pairs={{0,8},{4,12},{8,16},{12,20},{16,24},{20,28},{24,0},{28,4},{1,9},{5... | collective-permute-start | bytes 786440 | tf_op jit(solution)/shard_map/ppermute | solution.py:279
  33.1 10.0 %collective-permute-start.7 = (bf16[512,256]{1,0:T(8,128)(2,1)S(1)}, bf16[512,256]{1,0:T(8,128)(2,1)S(1)}, u32[]{:S(2)}, u32[]{:S(2)}) collective-permute-start(bf16[512,256]{1,0:T(8,128)(2,1)S(1)} %get-tuple-element.18), channel_id=1, source_target_pairs={{0,24},{4,28},{8,0},{12,4},{16,8},{20,12},{24,16},{28,20},{1,25},{... | collective-permute-start | bytes 786440 | tf_op jit(solution)/shard_map/ppermute | solution.py:279
  38.0 11.5 %collective-permute-start.12 = (bf16[256,2048]{1,0:T(8,128)(2,1)}, bf16[256,2048]{1,0:T(8,128)(2,1)S(1)}, u32[]{:S(2)}, u32[]{:S(2)}) collective-permute-start(bf16[256,2048]{1,0:T(8,128)(2,1)} %get-tuple-element.19), channel_id=1, source_target_pairs={{0,4},{4,0},{8,12},{12,8},{16,20},{20,16},{24,28},{28,24},{1,5},{5... | collective-permute-start | bytes 3145736 | tf_op jit(solution)/shard_map/ppermute | solution.py:282
  43.2 1.4 %collective-permute-start.8 = (bf16[256,256]{1,0:T(8,128)(2,1)S(1)}, bf16[256,256]{1,0:T(8,128)(2,1)S(1)}, u32[]{:S(2)}, u32[]{:S(2)}) collective-permute-start(bf16[256,256]{1,0:T(8,128)(2,1)S(1)} %get-tuple-element.34), channel_id=1, source_target_pairs={{0,4},{4,0},{8,12},{12,8},{16,20},{20,16},{24,28},{28,24},{1,5},{5... | collective-permute-start | bytes 393224 | tf_op jit(solution)/shard_map/ppermute | solution.py:282
  44.6 8.6 %collective-permute-start.10 = (bf16[64,512]{1,0:T(8,128)(2,1)S(1)}, bf16[64,512]{1,0:T(8,128)(2,1)S(1)}, u32[]{:S(2)}, u32[]{:S(2)}) collective-permute-start(bf16[64,512]{1,0:T(8,128)(2,1)S(1)} %get-tuple-element.33), channel_id=1, source_target_pairs={{0,2},{1,3},{2,0},{3,1},{4,6},{5,7},{6,4},{7,5},{8,10},{9,11},{10,... | collective-permute-start | bytes 196616 | tf_op jit(solution)/shard_map/ppermute | solution.py:276
  45.7 7.5 %collective-permute-start.11 = (bf16[64,512]{1,0:T(8,128)(2,1)S(1)}, bf16[64,512]{1,0:T(8,128)(2,1)S(1)}, u32[]{:S(2)}, u32[]{:S(2)}) collective-permute-start(bf16[64,512]{1,0:T(8,128)(2,1)S(1)} %get-tuple-element.30), channel_id=1, source_target_pairs={{0,1},{1,2},{2,3},{3,0},{4,5},{5,6},{6,7},{7,4},{8,9},{9,10},{10,1... | collective-permute-start | bytes 196616 | tf_op jit(solution)/shard_map/ppermute | solution.py:276
  48.2 5.4 %collective-permute-start.9 = (bf16[64,512]{1,0:T(8,128)(2,1)S(1)}, bf16[64,512]{1,0:T(8,128)(2,1)S(1)}, u32[]{:S(2)}, u32[]{:S(2)}) collective-permute-start(bf16[64,512]{1,0:T(8,128)(2,1)S(1)} %get-tuple-element.32), channel_id=1, source_target_pairs={{0,3},{1,0},{2,1},{3,2},{4,7},{5,4},{6,5},{7,6},{8,11},{9,8},{10,9... | collective-permute-start | bytes 196616 | tf_op jit(solution)/shard_map/ppermute | solution.py:276
  53.8 0.7 %copy-start.1 = (bf16[64,1024]{1,0:T(8,128)(2,1)}, bf16[64,1024]{1,0:T(8,128)(2,1)S(1)}, u32[]{:S(2)}) copy-start(bf16[64,1024]{1,0:T(8,128)(2,1)S(1)} %get-tuple-element.54) | copy-start | bytes 393220
  53.8 0.7 %copy-start = (bf16[64,1024]{1,0:T(8,128)(2,1)}, bf16[64,1024]{1,0:T(8,128)(2,1)S(1)}, u32[]{:S(2)}) copy-start(bf16[64,1024]{1,0:T(8,128)(2,1)S(1)} %slice_dynamic-update-slice_fusion.8) | copy-start | bytes 393220
